TPU v7x, 32 devices: a whole 2x2x4 slice. The times are simulated.
32 devices in a mesh: elem: 16 (over z, x, core), lev: 2 (over y).
Axes of the slice: x: 2, y: 2, z: 4, core: 2. Of those that a mesh axis runs over, the one named last changes fastest.
Arguments:
- zonal_wind: float32 [128, 16, 2048], P('lev', None, 'elem'), may hold values from -6 to 6
- meridional_wind: float32 [128, 16, 2048], P('lev', None, 'elem'), may hold values from -6 to 6
- vertical_wind: float32 [128, 16, 2048], P('lev', None, 'elem'), may hold values from -6 to 6
- pressure: float32 [128, 16, 2048], P('lev', None, 'elem'), may hold values from -6 to 6
- geopotential: float32 [128, 16, 2048], P('lev', None, 'elem'), may hold values from -6 to 6
- layer_mass: float32 [128, 16, 2048], P('lev', None, 'elem'), may hold values from 0.5 to 2
- stiffness: float32 [128, 16, 2048], P(None, 'lev', 'elem'), may hold values from 4 to 1024
- elem_order: int32 [16, 128], P('elem'), may hold values from 0 to 127, each once within a row
Outputs:
- zonal_out: float32 [128, 16, 2048], P('lev', None, 'elem')
- meridional_out: float32 [128, 16, 2048], P('lev', None, 'elem')
- vertical_out: float32 [128, 16, 2048], P('lev', None, 'elem')
- pressure_out: float32 [128, 16, 2048], P('lev', None, 'elem')
- geopotential_out: float32 [128, 16, 2048], P('lev', None, 'elem')
Inputs may be any that keep to these rules, and one draw needn't show every extreme that they name: `elem_order`: each row is a permutation of the positions 0 .. 127 of its strip.
All inputs are finite; a program needn't handle non-finite values.
Results may differ from a plain program's by a relative error of at most 0.0003.
Values sent between devices are 32-bit elements; how exact they have to be, the bound alone decides.
A program may use at most 128 MiB of HBM per device.

v0:
```python
import functools
import math

import jax
import jax.numpy as jnp
import numpy as np
from jax import lax
from jax.experimental import pallas as pl
from jax.experimental.pallas import tpu as pltpu
from jax.sharding import PartitionSpec as P

SUBSTEPS = 3


horizontal_speed = 0.12
drift_first = 0.1
drift_second = 0.06
geopotential_rate = 2.0


def padded(cells, sides, width):
    for axis, dim in sides:
        count = lax.axis_size(axis)
        head = lax.slice_in_dim(cells, 0, width, axis=dim)
        tail = lax.slice_in_dim(cells, cells.shape[dim] - width, cells.shape[dim], axis=dim)
        cells = jnp.concatenate(
            [
                lax.ppermute(tail, axis, [(i, (i + 1) % count) for i in range(count)]),
                cells,
                lax.ppermute(head, axis, [((i + 1) % count, i) for i in range(count)]),
            ],
            axis=dim,
        )
    return cells


def gll_tables():
    points = np.array([-1.0, -1.0 / math.sqrt(5.0), 1.0 / math.sqrt(5.0), 1.0])
    quadrature = np.array([1.0 / 6.0, 5.0 / 6.0, 5.0 / 6.0, 1.0 / 6.0])
    derivative = np.zeros((4, 4))
    for target in range(4):
        for source in range(4):
            if target == source:
                derivative[target, source] = sum(
                    (
                        1.0 / (points[target] - points[other])
                        for other in range(4)
                        if other != target
                    )
                )
            else:
                top_term = math.prod(
                    (points[target] - points[other] for other in range(4) if other != target)
                )
                low_term = math.prod(
                    (points[source] - points[other] for other in range(4) if other != source)
                )
                derivative[target, source] = top_term / (
                    low_term * (points[target] - points[source])
                )
    return (
        jnp.asarray(derivative, jnp.float32),
        jnp.asarray(np.outer(quadrature, quadrature).reshape(16), jnp.float32),
    )


def derivative_along(field, letters, which, derivative):
    result = letters.replace(which, "a")
    return jnp.einsum(
        "a" + which + "," + letters + "->" + result,
        derivative,
        field,
        precision=lax.Precision.HIGHEST,
    )


def assemble(stacked):
    axis_i, axis_j, axis_y = (2, 3, 4)
    left = lax.index_in_dim(stacked, 0, axis_i, keepdims=False)
    right = lax.index_in_dim(stacked, 3, axis_i, keepdims=False)
    faces = jnp.stack([left, right], 0)
    extended = padded(faces, (("elem", 0),), 1)
    left = left + extended[0]
    right = right + extended[3]
    stacked = jnp.concatenate(
        [
            jnp.expand_dims(left, axis_i),
            lax.slice_in_dim(stacked, 1, 3, axis=axis_i),
            jnp.expand_dims(right, axis_i),
        ],
        axis_i,
    )
    lower = lax.index_in_dim(stacked, 0, axis_j, keepdims=False)
    upper = lax.index_in_dim(stacked, 3, axis_j, keepdims=False)
    faces = jnp.stack([lower, upper], 0)
    length = faces.shape[axis_y]
    extended = jnp.concatenate(
        [
            lax.slice_in_dim(faces, length - 1, length, axis=axis_y),
            faces,
            lax.slice_in_dim(faces, 0, 1, axis=axis_y),
        ],
        axis_y,
    )
    lower = lower + lax.slice_in_dim(extended[1], 0, length, axis=axis_y - 1)
    upper = upper + lax.slice_in_dim(extended[0], 2, length + 2, axis=axis_y - 1)
    return jnp.concatenate(
        [
            jnp.expand_dims(lower, axis_j),
            lax.slice_in_dim(stacked, 1, 3, axis=axis_j),
            jnp.expand_dims(upper, axis_j),
        ],
        axis_j,
    )


def lift(field, stride, axis, fill):
    length = field.shape[axis]
    kept = lax.slice_in_dim(field, stride, length, axis=axis)
    padding = jnp.full_like(lax.slice_in_dim(field, 0, stride, axis=axis), fill)
    return jnp.concatenate([kept, padding], axis)


def sink(field, stride, axis, fill):
    length = field.shape[axis]
    kept = lax.slice_in_dim(field, 0, length - stride, axis=axis)
    padding = jnp.full_like(lax.slice_in_dim(field, 0, stride, axis=axis), fill)
    return jnp.concatenate([padding, kept], axis)


def column_step(upward, press, coeff, root, axis):
    rhs = upward - root * 0.5 * (lift(press, 1, axis, 0.0) - sink(press, 1, axis, 0.0))
    lower = -coeff
    upper = -coeff
    middle = 1.0 + 2.0 * coeff
    length = coeff.shape[axis]
    stride = 1
    while stride < length:
        from_below = -lower / sink(middle, stride, axis, 1.0)
        from_above = -upper / lift(middle, stride, axis, 1.0)
        new_lower = from_below * sink(lower, stride, axis, 0.0)
        new_upper = from_above * lift(upper, stride, axis, 0.0)
        middle = (
            middle
            + from_below * sink(upper, stride, axis, 0.0)
            + from_above * lift(lower, stride, axis, 0.0)
        )
        rhs = (
            rhs
            + from_below * sink(rhs, stride, axis, 0.0)
            + from_above * lift(rhs, stride, axis, 0.0)
        )
        lower, upper = (new_lower, new_upper)
        stride = stride * 2
    solved = rhs / middle
    press = press - root * 0.5 * (lift(solved, 1, axis, 0.0) - sink(solved, 1, axis, 0.0))
    return (solved, press)


def substep(state, mass, recip, letters, derivative, vertical):
    zonal, meridional, upward, press, geopot = state
    tendencies = jnp.stack(
        [
            mass * (-horizontal_speed * derivative_along(press, letters, "i", derivative)),
            mass * (-horizontal_speed * derivative_along(press, letters, "j", derivative)),
            mass
            * -(
                drift_first * derivative_along(upward, letters, "i", derivative)
                + drift_second * derivative_along(upward, letters, "j", derivative)
            ),
            mass
            * -(
                drift_first * derivative_along(geopot, letters, "i", derivative)
                + drift_second * derivative_along(geopot, letters, "j", derivative)
            ),
        ],
        0,
    )
    summed = assemble(tendencies)
    zonal = zonal + recip * summed[0]
    meridional = meridional + recip * summed[1]
    upward = upward + recip * summed[2]
    geopot = geopot + recip * summed[3]
    divergence = derivative_along(zonal, letters, "i", derivative) + derivative_along(
        meridional, letters, "j", derivative
    )
    press = press + recip * assemble(jnp.expand_dims(mass * (-horizontal_speed * divergence), 0))[0]
    solved, press = vertical(upward, press)
    geopot = geopot + geopotential_rate * solved
    return (zonal, meridional, solved, press, geopot)


def body(
    zonal_wind,
    meridional_wind,
    vertical_wind,
    pressure,
    geopotential,
    layer_mass,
    stiffness,
    elem_order,
):
    derivative, weights = gll_tables()
    order = elem_order[0]
    length = order.shape[0]
    inverse = jnp.zeros((length,), jnp.int32).at[order].set(jnp.arange(length, dtype=jnp.int32))
    levels = zonal_wind.shape[0]
    fields = [
        jnp.take(field, inverse, axis=2)
        for field in (zonal_wind, meridional_wind, vertical_wind, pressure, geopotential)
    ]
    mass = jnp.take(layer_mass, inverse, axis=2) * weights[None, :, None]
    coeff_grid = jnp.take(stiffness, inverse, axis=2)
    grid_mass = mass.reshape(levels, 4, 4, length)
    recip = 1.0 / assemble(jnp.expand_dims(grid_mass, 0))[0]
    root_grid = jnp.sqrt(coeff_grid)

    def vertical(upward, press):
        stacked = jnp.stack([upward, press], 0).reshape(2, levels, 16, length)
        columns = lax.all_to_all(stacked, "lev", split_axis=2, concat_axis=1, tiled=True)
        solved, press_new = column_step(columns[0], columns[1], coeff_grid, root_grid, 0)
        back = lax.all_to_all(
            jnp.stack([solved, press_new], 0), "lev", split_axis=1, concat_axis=2, tiled=True
        )
        back = back.reshape(2, levels, 4, 4, length)
        return (back[0], back[1])

    state = tuple((field.reshape(levels, 4, 4, length) for field in fields))
    for step in range(SUBSTEPS):
        state = substep(state, grid_mass, recip, "lijy", derivative, vertical)
    results = [field.reshape(levels, 16, length) for field in state]
    outputs = [jnp.take(field, order, axis=2) for field in results]
    return (outputs[0], outputs[1], outputs[2], outputs[3], outputs[4])


CHUNKS = 2
TILE = 8


def derivative_parts():
    points = np.array([-1.0, -1.0 / math.sqrt(5.0), 1.0 / math.sqrt(5.0), 1.0])
    matrix = np.zeros((4, 4))
    for a in range(4):
        for b in range(4):
            if a == b:
                matrix[a, b] = sum(1.0 / (points[a] - points[o]) for o in range(4) if o != a)
            else:
                top = math.prod(points[a] - points[o] for o in range(4) if o != a)
                low = math.prod(points[b] - points[o] for o in range(4) if o != b)
                matrix[a, b] = top / (low * (points[a] - points[b]))
    return matrix


MATRIX = derivative_parts()


def line(f0, f1, f2, f3, scale):
    outer, inner = f0 - f3, f1 - f2
    bend = (f0 + f3) - (f1 + f2)
    out = [None] * 4
    for a in (0, 1):
        m = MATRIX[a] * scale
        odd = float(0.5 * (m[0] - m[3])) * outer + float(0.5 * (m[1] - m[2])) * inner
        even = float(0.5 * (m[0] + m[3])) * bend
        out[a], out[3 - a] = odd + even, odd - even
    return out


def along_i(f, scale):
    out = [None] * 16
    for j in range(4):
        for i, value in enumerate(line(f[j], f[4 + j], f[8 + j], f[12 + j], scale)):
            out[4 * i + j] = value
    return out


def along_j(f, scale):
    out = [None] * 16
    for i in range(4):
        out[4 * i : 4 * i + 4] = line(*f[4 * i : 4 * i + 4], scale)
    return out


def ahead(x):
    return pltpu.roll(x, x.shape[1] - 1, 1)


def behind(x):
    return pltpu.roll(x, 1, 1)


def join_j(f):
    out = list(f)
    for i in range(4):
        shared = f[4 * i + 3] + ahead(f[4 * i])
        out[4 * i + 3] = shared
        out[4 * i] = behind(shared)
    return out


def lanes(x, index):
    return jnp.take_along_axis(x, index, axis=1, mode="promise_in_bounds")


def fused(
    strips,
    zon, mer, ver, pre, geo, lay, stf, inv_ref, ord_ref,
    o_zon, o_mer, o_ver, o_pre, o_geo,
    U, V, G, M, R, P, W, Z, C, I, H, A,
    s_m, r_m, s_uv, r_uv, s_w, r_w, s_d, r_d, s_g, r_g, s_e, r_e, r_a,
    send_sem, recv_sem,
):
    levels = U.shape[1]
    span = levels // CHUNKS
    tiles = span // TILE
    me = lax.axis_index("elem")
    lev = lax.axis_index("lev")
    left, right = lax.rem(me + strips - 1, strips), lax.rem(me + 1, strips)
    other = 1 - lev
    inv = inv_ref[...]
    order = ord_ref[...]
    quad = [1.0 / 6.0, 5.0 / 6.0, 5.0 / 6.0, 1.0 / 6.0]
    weights = [quad[n // 4] * quad[n % 4] for n in range(16)]
    started = []
    MESH = pl.DeviceIdType.MESH

    def send(src, dst, target):
        slot = len(started)
        copy = pltpu.make_async_remote_copy(
            src_ref=src, dst_ref=dst, send_sem=send_sem.at[slot], recv_sem=recv_sem.at[slot],
            device_id=target, device_id_type=MESH,
        )
        copy.start()
        started.append(copy)
        return copy

    def send_faces(out, back, step, c):
        return [
            send(out.at[step, 0, c], back.at[step, 0, c], {"elem": left}),
            send(out.at[step, 1, c], back.at[step, 1, c], {"elem": right}),
        ]

    def arrive(copies):
        for copy in copies:
            copy.wait_recv()

    def column_rows(n, l0):
        return (pl.ds(l0 * 16 + n, TILE, stride=16), slice(None))

    def node_rows(n, l0):
        return (n, pl.ds(l0, TILE), slice(None))

    def each_tile(c, work):
        def go(b, carry):
            work(pl.multiple_of(c * span + b * TILE, TILE), pl.multiple_of(b * TILE, TILE))
            return carry

        lax.fori_loop(0, tiles, go, 0)

    def put_faces(buf, step, c, at, b0, f):
        for j in range(3):
            buf[step, 0, c, at + j, pl.ds(b0, TILE), :] = f[j]
            buf[step, 1, c, at + j, pl.ds(b0, TILE), :] = f[12 + j]

    def total_faces(out, back, step, c, at, b0):
        result = {}
        for i, own, theirs in ((0, 0, 1), (3, 1, 0)):
            for j in range(3):
                result[4 * i + j] = (
                    out[step, own, c, at + j, pl.ds(b0, TILE), :]
                    + back[step, theirs, c, at + j, pl.ds(b0, TILE), :]
                )
            result[4 * i + 3] = ahead(result[4 * i])
        return result

    barrier = pltpu.get_barrier_semaphore()
    for target in ({"elem": left}, {"elem": right}, {"lev": other}):
        pl.semaphore_signal(barrier, inc=1, device_id=target, device_id_type=MESH)
    pl.semaphore_wait(barrier, 3)

    stiff_copy = send(stf.at[pl.ds(pl.multiple_of(other * levels, 8), levels)], r_a, {"lev": other})

    def gather_rows(src, dst, c):
        def go(b, carry):
            for q in range(16):
                at = pl.ds(pl.multiple_of(c * span * 16 + b * 128 + q * 8, 8), 8)
                dst[at, :] = lanes(src[at, :], inv)
            return carry

        lax.fori_loop(0, tiles, go, 0)

    def load_mass(c):
        def work(l0, b0):
            m = [lanes(lay[column_rows(n, l0)], inv) * weights[n] for n in range(16)]
            for n in range(16):
                M[node_rows(n, l0)] = m[n]
            m = join_j(m)
            for n in range(4, 12):
                R[node_rows(n, l0)] = 1.0 / m[n]
            put_faces(s_m, 0, c, 0, b0, m)

        each_tile(c, work)

    def wind_step(step, c):
        def work(l0, b0):
            p = [P[column_rows(n, l0)] for n in range(16)]
            m = [M[node_rows(n, l0)] for n in range(16)]
            for at, field, d in ((0, U, along_i), (3, V, along_j)):
                t = join_j([x * y for x, y in zip(m, d(p, -horizontal_speed))])
                for n in range(4, 12):
                    add = R[node_rows(n, l0)] * t[n]
                    field[node_rows(n, l0)] = add if step == 0 else field[node_rows(n, l0)] + add
                put_faces(s_uv, step, c, at, b0, t)

        each_tile(c, work)

    def start_winds(c):
        def work(l0, b0):
            for src, field in ((zon, U), (mer, V)):
                for n in range(16):
                    value = lanes(src[column_rows(n, l0)], inv)
                    if 4 <= n < 12:
                        value = value + field[node_rows(n, l0)]
                    field[node_rows(n, l0)] = value

        each_tile(c, work)

    def drift(f, m):
        first, second = along_i(f, -drift_first), along_j(f, -drift_second)
        return join_j([k * (x + y) for k, x, y in zip(m, first, second)])

    def vertical_step(step, c):
        def work(l0, b0):
            m = [M[node_rows(n, l0)] for n in range(16)]
            w = [W[column_rows(n, l0)] for n in range(16)]
            for n in range(16):
                if step == 0:
                    G[node_rows(n, l0)] = lanes(geo[column_rows(n, l0)], inv)
                else:
                    G[node_rows(n, l0)] = G[node_rows(n, l0)] + geopotential_rate * w[n]
            t = drift(w, m)
            for n in range(4, 12):
                W[column_rows(n, l0)] = w[n] + R[node_rows(n, l0)] * t[n]
            put_faces(s_w, step, c, 0, b0, t)

        each_tile(c, work)

    def geopotential_step(step, c):
        def work(l0, b0):
            m = [M[node_rows(n, l0)] for n in range(16)]
            g = [G[node_rows(n, l0)] for n in range(16)]
            t = drift(g, m)
            for n in range(4, 12):
                G[node_rows(n, l0)] = g[n] + R[node_rows(n, l0)] * t[n]
            put_faces(s_g, step, c, 0, b0, t)

        each_tile(c, work)

    def mass_faces(c):
        def work(l0, b0):
            for n, total in total_faces(s_m, r_m, 0, c, 0, b0).items():
                R[node_rows(n, l0)] = 1.0 / total

        each_tile(c, work)

    def divergence_step(step, c):
        def work(l0, b0):
            for at, field in ((0, U), (3, V)):
                for n, total in total_faces(s_uv, r_uv, step, c, at, b0).items():
                    field[node_rows(n, l0)] = field[node_rows(n, l0)] + R[node_rows(n, l0)] * total
            m = [M[node_rows(n, l0)] for n in range(16)]
            du = along_i([U[node_rows(n, l0)] for n in range(16)], -horizontal_speed)
            dv = along_j([V[node_rows(n, l0)] for n in range(16)], -horizontal_speed)
            t = join_j([k * (x + y) for k, x, y in zip(m, du, dv)])
            for n in range(4, 12):
                P[column_rows(n, l0)] = P[column_rows(n, l0)] + R[node_rows(n, l0)] * t[n]
            put_faces(s_d, step, c, 0, b0, t)

        each_tile(c, work)

    def column_faces(field, out, back, step, c):
        def work(l0, b0):
            for n, total in total_faces(out, back, step, c, 0, b0).items():
                field[column_rows(n, l0)] = field[column_rows(n, l0)] + R[node_rows(n, l0)] * total

        each_tile(c, work)

    def geopotential_faces(step, c):
        def work(l0, b0):
            for n, total in total_faces(s_g, r_g, step, c, 0, b0).items():
                G[node_rows(n, l0)] = G[node_rows(n, l0)] + R[node_rows(n, l0)] * total

        each_tile(c, work)

    def row(e):
        k = e + lev * (levels - 1 - 2 * e)
        return pl.ds(pl.multiple_of(k * 16, 16), 16)

    side = (1 - 2 * lev).astype(jnp.float32)
    zero = jnp.zeros((16, P.shape[1]), jnp.float32)

    def factor():
        def fill(k, carry):
            mine = lanes(stf[lev * levels + k], inv)
            theirs = lanes(r_a[k], inv)
            top = jnp.where(lev == 0, mine, theirs)
            bottom = jnp.where(lev == 0, theirs, mine)
            both = jnp.concatenate([top, bottom], 0)
            at = pl.ds(pl.multiple_of(k * 16, 16), 16)
            A[at, :] = both
            H[at, :] = jnp.sqrt(both) * (0.5 * side)
            return carry

        lax.fori_loop(0, levels, fill, 0, unroll=4)

        def go(block, ratio):
            for u in range(4):
                at = row(block * 4 + u)
                a = A[at, :]
                turn = 1.0 / (1.0 + 2.0 * a - a * ratio)
                ratio = a * turn
                C[at, :] = ratio
                I[at, :] = turn
            return ratio

        lax.fori_loop(0, levels // 4, go, zero)
        at = row(levels - 1)
        s_e[0, 0] = C[at, :]
        s_e[0, 1] = H[at, :] * I[at, :]
        return send(s_e.at[0], r_e.at[0], {"lev": other})

    def eliminate(step):
        def one(e, before, here, after, z):
            at = row(e)
            z = (W[at, :] - H[at, :] * (after - before)) * I[at, :] + C[at, :] * z
            Z[at, :] = z
            return here, after, z

        def go(block, carry):
            before, here, z = carry
            for u in range(8):
                e = block * 8 + u
                after = P[row(e + 1), :]
                before, here, z = one(e, before, here, after, z)
            return before, here, z

        carry = lax.fori_loop(0, levels // 8 - 1, go, (zero, P[row(0), :], zero))
        before, here, z = carry
        for u in range(8):
            e = levels - 8 + u
            after = P[row(e + 1), :] if u < 7 else zero
            before, here, z = one(e, before, here, after, z)
        s_e[step + 1, 0] = z
        s_e[step + 1, 1] = before
        return send(s_e.at[step + 1], r_e.at[step + 1], {"lev": other})

    def substitute(step):
        ratio, pull = s_e[0, 0], s_e[0, 1]
        ratio_other, pull_other = r_e[0, 0], r_e[0, 1]
        z = s_e[step + 1, 0] - pull * r_e[step + 1, 1]
        z_other = r_e[step + 1, 0] - pull_other * s_e[step + 1, 1]
        x = (z + ratio * z_other) / (1.0 - ratio * ratio_other)
        beyond = z_other + ratio_other * x
        W[row(levels - 1), :] = x

        def one(e, beyond, x):
            here = Z[row(e), :] + C[row(e), :] * x
            W[row(e), :] = here
            at = row(e + 1)
            P[at, :] = P[at, :] - H[at, :] * (beyond - here)
            return x, here

        carry = (beyond, x)
        for u in range(7):
            carry = one(levels - 2 - u, *carry)

        def go(block, carry):
            for u in range(8):
                carry = one(levels - 9 - block * 8 - u, *carry)
            return carry

        beyond, x = lax.fori_loop(0, levels // 8 - 1, go, carry)
        at = row(0)
        P[at, :] = P[at, :] - H[at, :] * beyond

    def write_nodes(field, out, c):
        def work(l0, b0):
            for n in range(16):
                out[column_rows(n, l0)] = lanes(field[node_rows(n, l0)], order)

        each_tile(c, work)

    def write_geopotential(c):
        def work(l0, b0):
            for n in range(16):
                value = G[node_rows(n, l0)] + geopotential_rate * W[column_rows(n, l0)]
                o_geo[column_rows(n, l0)] = lanes(value, order)

        each_tile(c, work)

    def write_rows(field, out):
        def go(b, carry):
            for q in range(16):
                at = pl.ds(pl.multiple_of(b * 128 + q * 8, 8), 8)
                out[at, :] = lanes(field[at, :], order)
            return carry

        lax.fori_loop(0, levels // TILE, go, 0)

    edge_copy = None
    for step in range(SUBSTEPS):
        uv, w, d, g, m = [], [], [], [], []
        for c in range(CHUNKS):
            if step == 0:
                load_mass(c)
                m.append(send_faces(s_m, r_m, 0, c))
                gather_rows(pre, P, c)
            wind_step(step, c)
            uv.append(send_faces(s_uv, r_uv, step, c))
        for c in range(CHUNKS):
            if step == 0:
                gather_rows(ver, W, c)
            vertical_step(step, c)
            w.append(send_faces(s_w, r_w, step, c))
        if step == 0:
            for c in range(CHUNKS):
                start_winds(c)
                arrive(m[c])
                mass_faces(c)
        for c in range(CHUNKS):
            arrive(uv[c])
            divergence_step(step, c)
            d.append(send_faces(s_d, r_d, step, c))
        for c in range(CHUNKS):
            geopotential_step(step, c)
            g.append(send_faces(s_g, r_g, step, c))
        if step == 0:
            stiff_copy.wait_recv()
            edge_copy = factor()
        if step == SUBSTEPS - 1:
            for c in range(CHUNKS):
                write_nodes(U, o_zon, c)
                write_nodes(V, o_mer, c)
        for c in range(CHUNKS):
            arrive(w[c])
            column_faces(W, s_w, r_w, step, c)
        for c in range(CHUNKS):
            arrive(d[c])
            column_faces(P, s_d, r_d, step, c)
        message = eliminate(step)
        for c in range(CHUNKS):
            arrive(g[c])
            geopotential_faces(step, c)
        if step == 0:
            edge_copy.wait_recv()
        message.wait_recv()
        substitute(step)
    for c in range(CHUNKS):
        write_geopotential(c)
    write_rows(W, o_ver)
    write_rows(P, o_pre)
    for copy in started:
        copy.wait_send()


def pair_step(
    strips, zonal_wind, meridional_wind, vertical_wind, pressure, geopotential, layer_mass,
    stiffness, elem_order,
):
    levels, nodes, length = zonal_wind.shape
    order = elem_order[0]
    slots = jnp.arange(length, dtype=jnp.int32)
    inverse = jnp.sum(jnp.where(order[:, None] == slots[None, :], slots[:, None], 0), axis=0)
    inv = jnp.broadcast_to(inverse[None, :], (TILE, length))
    back = jnp.broadcast_to(elem_order, (TILE, length))
    fields = [
        f.reshape(levels * nodes, length)
        for f in (zonal_wind, meridional_wind, vertical_wind, pressure, geopotential, layer_mass)
    ]
    span = levels // CHUNKS

    def faces(steps, count):
        return [pltpu.VMEM((steps, 2, CHUNKS, count, span, length), jnp.float32)] * 2

    node_major = pltpu.VMEM((nodes, levels, length), jnp.float32)
    level_major = pltpu.VMEM((levels * nodes, length), jnp.float32)
    edges = pltpu.VMEM((SUBSTEPS + 1, 2, nodes, length), jnp.float32)
    copies = 1 + 2 * CHUNKS + SUBSTEPS * 8 * CHUNKS + 1 + SUBSTEPS
    vmem = pl.BlockSpec(memory_space=pltpu.VMEM)
    outputs = pl.pallas_call(
        functools.partial(fused, strips),
        out_shape=[jax.ShapeDtypeStruct((levels * nodes, length), jnp.float32)] * 5,
        in_specs=[vmem] * 9,
        out_specs=[vmem] * 5,
        scratch_shapes=[node_major] * 5
        + [level_major] * 7
        + faces(1, 3)
        + faces(SUBSTEPS, 6)
        + faces(SUBSTEPS, 3)
        + faces(SUBSTEPS, 3)
        + faces(SUBSTEPS, 3)
        + [edges, edges, pltpu.VMEM((levels, nodes // 2, length), jnp.float32)]
        + [pltpu.SemaphoreType.DMA((copies,)), pltpu.SemaphoreType.DMA((copies,))],
        compiler_params=pltpu.CompilerParams(
            collective_id=0, has_side_effects=True, vmem_limit_bytes=40 * 1024 * 1024
        ),
        name="acoustic_substeps",
    )(*fields, stiffness, inv, back)
    return tuple(f.reshape(levels, nodes, length) for f in outputs)


def local_step(strips, pair, *arrays):
    levels, nodes, length = arrays[0].shape
    if pair == 2 and strips > 2 and nodes == 16 and length == 128 and levels % (CHUNKS * TILE) == 0:
        return pair_step(strips, *arrays)
    return body(*arrays)


def solution(mesh):
    placed = (
        P("lev", None, "elem"),
        P("lev", None, "elem"),
        P("lev", None, "elem"),
        P("lev", None, "elem"),
        P("lev", None, "elem"),
        P("lev", None, "elem"),
        P(None, "lev", "elem"),
        P("elem", None),
    )
    return jax.shard_map(
        functools.partial(local_step, mesh.shape["elem"], mesh.shape["lev"]),
        mesh=mesh,
        in_specs=placed,
        out_specs=(
            P("lev", None, "elem"),
            P("lev", None, "elem"),
            P("lev", None, "elem"),
            P("lev", None, "elem"),
            P("lev", None, "elem"),
        ),
        check_vma=False,
    )
```

profile of v0, /device:TPU:1, one launch (start us, length us, event | category | flops | bytes accessed | tf_op | source)
XLA Modules:
  0.0 69.0 jit_solution(15956246129514016510)
XLA Ops:
  0.6 0.0 copy-start.7
  0.6 0.6 copy-done.7
  1.3 0.1 select_reduce_fusion
  1.4 0.0 copy-start
  1.4 1.0 %copy-done = f32[64,16,128]{2,1,0:T(8,128)S(1)} copy-done((f32[64,16,128]{2,1,0:T(8,128)S(1)}, f32[64,16,128]{2,1,0:T(8,128)}, u32[]{:S(2)}) %copy-start) | copy-done | bytes 524312
  2.4 0.0 copy-start.1
  2.5 1.0 %copy-done.1 = f32[64,16,128]{2,1,0:T(8,128)S(1)} copy-done((f32[64,16,128]{2,1,0:T(8,128)S(1)}, f32[64,16,128]{2,1,0:T(8,128)}, u32[]{:S(2)}) %copy-start.1) | copy-done | bytes 524312
  3.5 0.0 copy-start.2
  3.5 1.0 %copy-done.2 = f32[64,16,128]{2,1,0:T(8,128)S(1)} copy-done((f32[64,16,128]{2,1,0:T(8,128)S(1)}, f32[64,16,128]{2,1,0:T(8,128)}, u32[]{:S(2)}) %copy-start.2) | copy-done | bytes 524312
  4.5 0.0 copy-start.3
  4.5 1.0 %copy-done.3 = f32[64,16,128]{2,1,0:T(8,128)S(1)} copy-done((f32[64,16,128]{2,1,0:T(8,128)S(1)}, f32[64,16,128]{2,1,0:T(8,128)}, u32[]{:S(2)}) %copy-start.3) | copy-done | bytes 524312
  5.6 0.0 copy-start.4
  5.6 1.0 %copy-done.4 = f32[64,16,128]{2,1,0:T(8,128)S(1)} copy-done((f32[64,16,128]{2,1,0:T(8,128)S(1)}, f32[64,16,128]{2,1,0:T(8,128)}, u32[]{:S(2)}) %copy-start.4) | copy-done | bytes 524312
  6.6 0.0 copy-start.5
  6.6 1.0 %copy-done.5 = f32[64,16,128]{2,1,0:T(8,128)S(1)} copy-done((f32[64,16,128]{2,1,0:T(8,128)S(1)}, f32[64,16,128]{2,1,0:T(8,128)}, u32[]{:S(2)}) %copy-start.5) | copy-done | bytes 524312
  7.7 0.0 copy-start.6
  7.7 1.0 %copy-done.6 = f32[128,8,128]{2,1,0:T(8,128)S(1)} copy-done((f32[128,8,128]{2,1,0:T(8,128)S(1)}, f32[128,8,128]{2,1,0:T(8,128)}, u32[]{:S(2)}) %copy-start.6) | copy-done | bytes 524312
  8.7 56.4 %acoustic_substeps.1 = (f32[1024,128]{1,0:T(8,128)S(1)}, f32[1024,128]{1,0:T(8,128)S(1)}, f32[1024,128]{1,0:T(8,128)S(1)}, f32[1024,128]{1,0:T(8,128)S(1)}, f32[1024,128]{1,0:T(8,128)S(1)}) custom-call(f32[1024,128]{1,0:T(8,128)S(1)} %bitcast.12, f32[1024,128]{1,0:T(8,128)S(1)} %bitcast.13, f32[1024,128]{1,0:T(8,128)S(1)} %bitcast.14, ...), custom_call_target="tpu_custom_call" | custom-call | tf_op jit(solution)/shard_map/acoustic_substeps/pallas_call | solution.py:690
  65.1 0.8 %copy.18 = f32[64,16,128]{2,1,0:T(8,128)} copy(f32[64,16,128]{2,1,0:T(8,128)S(1)} %bitcast.22) | data formatting | bytes 1048576
  65.9 0.8 %copy.19 = f32[64,16,128]{2,1,0:T(8,128)} copy(f32[64,16,128]{2,1,0:T(8,128)S(1)} %bitcast.21) | data formatting | bytes 1048576
  66.7 0.8 %copy.20 = f32[64,16,128]{2,1,0:T(8,128)} copy(f32[64,16,128]{2,1,0:T(8,128)S(1)} %bitcast.20) | data formatting | bytes 1048576
  67.5 0.8 %copy.21 = f32[64,16,128]{2,1,0:T(8,128)} copy(f32[64,16,128]{2,1,0:T(8,128)S(1)} %bitcast.19) | data formatting | bytes 1048576
  68.3 0.8 %copy.22 = f32[64,16,128]{2,1,0:T(8,128)} copy(f32[64,16,128]{2,1,0:T(8,128)S(1)} %bitcast.18) | data formatting | bytes 1048576
  (2 shorter events, 0.0 us)
Async XLA Ops:
  0.6 0.7 copy-start.7
  1.4 1.0 %copy-start = (f32[64,16,128]{2,1,0:T(8,128)S(1)}, f32[64,16,128]{2,1,0:T(8,128)}, u32[]{:S(2)}) copy-start(f32[64,16,128]{2,1,0:T(8,128)} %param.8) | copy-start | bytes 1572868
  2.4 1.0 %copy-start.1 = (f32[64,16,128]{2,1,0:T(8,128)S(1)}, f32[64,16,128]{2,1,0:T(8,128)}, u32[]{:S(2)}) copy-start(f32[64,16,128]{2,1,0:T(8,128)} %param.9) | copy-start | bytes 1572868
  3.5 1.0 %copy-start.2 = (f32[64,16,128]{2,1,0:T(8,128)S(1)}, f32[64,16,128]{2,1,0:T(8,128)}, u32[]{:S(2)}) copy-start(f32[64,16,128]{2,1,0:T(8,128)} %param.10) | copy-start | bytes 1572868
  4.5 1.0 %copy-start.3 = (f32[64,16,128]{2,1,0:T(8,128)S(1)}, f32[64,16,128]{2,1,0:T(8,128)}, u32[]{:S(2)}) copy-start(f32[64,16,128]{2,1,0:T(8,128)} %param.11) | copy-start | bytes 1572868
  5.6 1.0 %copy-start.4 = (f32[64,16,128]{2,1,0:T(8,128)S(1)}, f32[64,16,128]{2,1,0:T(8,128)}, u32[]{:S(2)}) copy-start(f32[64,16,128]{2,1,0:T(8,128)} %param.12) | copy-start | bytes 1572868
  6.6 1.0 %copy-start.5 = (f32[64,16,128]{2,1,0:T(8,128)S(1)}, f32[64,16,128]{2,1,0:T(8,128)}, u32[]{:S(2)}) copy-start(f32[64,16,128]{2,1,0:T(8,128)} %param.13) | copy-start | bytes 1572868
  7.7 1.0 %copy-start.6 = (f32[128,8,128]{2,1,0:T(8,128)S(1)}, f32[128,8,128]{2,1,0:T(8,128)}, u32[]{:S(2)}) copy-start(f32[128,8,128]{2,1,0:T(8,128)} %stf.1) | copy-start | bytes 1572868
where the time goes:
time: 69.5 us; the launch traced here: 69 us
  Pallas kernels  56.4 us (81%)
  local copies, waits for them, and re-layouts  11.9 us (17%)
    pallas_call x1, Pallas kernels, pair_step(): pl.pallas_call(functools.partial(fused, strips), out_shape=[jax.ShapeDtyp...  56.4 us
    unnamed x21, local copies, waits for them, and re-layouts  11.9 us

commit v1 on v0

--- a/solution.py
+++ b/solution.py
@@ -304,11 +304,11 @@
 
 def fused(
     strips,
-    zon, mer, ver, pre, geo, lay, stf, inv_ref, ord_ref,
+    h_zon, h_mer, h_ver, h_pre, h_geo, h_lay, h_stf, inv_ref, ord_ref,
     o_zon, o_mer, o_ver, o_pre, o_geo,
     U, V, G, M, R, P, W, Z, C, I, H, A,
     s_m, r_m, s_uv, r_uv, s_w, r_w, s_d, r_d, s_g, r_g, s_e, r_e, r_a,
-    send_sem, recv_sem,
+    zon, mer, ver, pre, geo, lay, stf, send_sem, recv_sem, load_sem,
 ):
     levels = U.shape[1]
     span = levels // CHUNKS
@@ -373,12 +373,33 @@
             result[4 * i + 3] = ahead(result[4 * i])
         return result
 
+    def fetch(src, dst, slot):
+        half = dst.shape[0] // 2
+        copies = []
+        for part in range(2):
+            rows = pl.ds(part * half, half)
+            copy = pltpu.make_async_copy(src.at[rows], dst.at[rows], load_sem.at[2 * slot + part])
+            copy.start()
+            copies.append(copy)
+        return copies
+
+    def loaded(copies):
+        for copy in copies:
+            copy.wait()
+
+    lay_in, pre_in = fetch(h_lay, lay, 0), fetch(h_pre, pre, 1)
+    ver_in, geo_in = fetch(h_ver, ver, 2), fetch(h_geo, geo, 3)
+    zon_in, mer_in = fetch(h_zon, zon, 4), fetch(h_mer, mer, 5)
+    own = pl.ds(pl.multiple_of(lev * levels, 8), levels)
+    stf_in = pltpu.make_async_copy(h_stf.at[own], stf, load_sem.at[12])
+    stf_in.start()
+
     barrier = pltpu.get_barrier_semaphore()
     for target in ({"elem": left}, {"elem": right}, {"lev": other}):
         pl.semaphore_signal(barrier, inc=1, device_id=target, device_id_type=MESH)
     pl.semaphore_wait(barrier, 3)
 
-    stiff_copy = send(stf.at[pl.ds(pl.multiple_of(other * levels, 8), levels)], r_a, {"lev": other})
+    stiff_copy = send(h_stf.at[pl.ds(pl.multiple_of(other * levels, 8), levels)], r_a, {"lev": other})
 
     def gather_rows(src, dst, c):
         def go(b, carry):
@@ -501,7 +522,7 @@
 
     def factor():
         def fill(k, carry):
-            mine = lanes(stf[lev * levels + k], inv)
+            mine = lanes(stf[k], inv)
             theirs = lanes(r_a[k], inv)
             top = jnp.where(lev == 0, mine, theirs)
             bottom = jnp.where(lev == 0, theirs, mine)
@@ -612,17 +633,24 @@
         uv, w, d, g, m = [], [], [], [], []
         for c in range(CHUNKS):
             if step == 0:
+                if c == 0:
+                    loaded(lay_in)
                 load_mass(c)
                 m.append(send_faces(s_m, r_m, 0, c))
+                if c == 0:
+                    loaded(pre_in)
                 gather_rows(pre, P, c)
             wind_step(step, c)
             uv.append(send_faces(s_uv, r_uv, step, c))
         for c in range(CHUNKS):
             if step == 0:
+                if c == 0:
+                    loaded(ver_in + geo_in)
                 gather_rows(ver, W, c)
             vertical_step(step, c)
             w.append(send_faces(s_w, r_w, step, c))
         if step == 0:
+            loaded(zon_in + mer_in)
             for c in range(CHUNKS):
                 start_winds(c)
                 arrive(m[c])
@@ -635,6 +663,7 @@
             geopotential_step(step, c)
             g.append(send_faces(s_g, r_g, step, c))
         if step == 0:
+            stf_in.wait()
             stiff_copy.wait_recv()
             edge_copy = factor()
         if step == SUBSTEPS - 1:
@@ -663,6 +692,19 @@
         copy.wait_send()
 
 
+def store(a, b, c, d, e, p, q, r, s, t, sem):
+    copies = []
+    for src, dst in ((a, p), (b, q), (c, r), (d, s), (e, t)):
+        half = src.shape[0] // 2
+        for part in range(2):
+            rows = pl.ds(part * half, half)
+            copy = pltpu.make_async_copy(src.at[rows], dst.at[rows], sem.at[len(copies)])
+            copy.start()
+            copies.append(copy)
+    for copy in copies:
+        copy.wait()
+
+
 def pair_step(
     strips, zonal_wind, meridional_wind, vertical_wind, pressure, geopotential, layer_mass,
     stiffness, elem_order,
@@ -689,8 +731,8 @@
     vmem = pl.BlockSpec(memory_space=pltpu.VMEM)
     outputs = pl.pallas_call(
         functools.partial(fused, strips),
-        out_shape=[jax.ShapeDtypeStruct((levels * nodes, length), jnp.float32)] * 5,
-        in_specs=[vmem] * 9,
+        out_shape=[pltpu.VMEM((levels * nodes, length), jnp.float32)] * 5,
+        in_specs=[pl.BlockSpec(memory_space=pltpu.HBM)] * 7 + [vmem] * 2,
         out_specs=[vmem] * 5,
         scratch_shapes=[node_major] * 5
         + [level_major] * 7
@@ -700,12 +742,23 @@
         + faces(SUBSTEPS, 3)
         + faces(SUBSTEPS, 3)
         + [edges, edges, pltpu.VMEM((levels, nodes // 2, length), jnp.float32)]
-        + [pltpu.SemaphoreType.DMA((copies,)), pltpu.SemaphoreType.DMA((copies,))],
+        + [level_major] * 6
+        + [pltpu.VMEM((levels, nodes // 2, length), jnp.float32)]
+        + [pltpu.SemaphoreType.DMA((copies,)), pltpu.SemaphoreType.DMA((copies,))]
+        + [pltpu.SemaphoreType.DMA((13,))],
         compiler_params=pltpu.CompilerParams(
-            collective_id=0, has_side_effects=True, vmem_limit_bytes=40 * 1024 * 1024
+            collective_id=0, has_side_effects=True, vmem_limit_bytes=52 * 1024 * 1024
         ),
         name="acoustic_substeps",
     )(*fields, stiffness, inv, back)
+    outputs = pl.pallas_call(
+        store,
+        out_shape=[jax.ShapeDtypeStruct((levels * nodes, length), jnp.float32)] * 5,
+        in_specs=[vmem] * 5,
+        out_specs=[pl.BlockSpec(memory_space=pl.ANY)] * 5,
+        scratch_shapes=[pltpu.SemaphoreType.DMA((10,))],
+        name="store_outputs",
+    )(*outputs)
     return tuple(f.reshape(levels, nodes, length) for f in outputs)
 
 

time: 69.5 us -> 67.1 us (0.965)
  local copies, waits for them, and re-layouts: 11.9 us -> 5.79 us
  Pallas kernels: 56.4 us -> 60.3 us
    unnamed x21 -> x12, local copies, waits for them, and re-layouts: 11.9 us -> 4.6 us
    pallas_call x1 -> x2, Pallas kernels: 56.4 us -> 60.3 us  [the longest x1 57.1 us: pair_step(): pl.pallas_call(functools.partial(fused, strips), out_shape=[pltpu.VMEM((l...]
where the time goes in v1:
time: 67.1 us; the launch traced here: 66.9 us
  Pallas kernels  60.3 us (90%)
  local copies, waits for them, and re-layouts  5.79 us (9%)
    pallas_call x1, Pallas kernels, pair_step(): pl.pallas_call(functools.partial(fused, strips), out_shape=[pltpu.VMEM((l...  57.1 us
    unnamed x12, local copies, waits for them, and re-layouts  4.6 us
    pallas_call x1, Pallas kernels, pair_step(): pl.pallas_call(store, out_shape=[jax.ShapeDtypeStruct((levels * nodes, le...  3.24 us

profile of v1, /device:TPU:1, one launch (start us, length us, event | category | flops | bytes accessed | tf_op | source)
XLA Modules:
  0.0 66.9 jit_solution(12701186926319966927)
XLA Ops:
  0.6 0.0 copy-start.5
  0.6 0.6 copy-done.5
  1.3 0.1 select_reduce_fusion
  1.4 0.6 broadcast_in_dim.27.inv_ref
  2.0 0.6 broadcast_in_dim.28.ord_ref
  2.6 57.1 %acoustic_substeps.1 = (f32[1024,128]{1,0:T(8,128)S(1)}, f32[1024,128]{1,0:T(8,128)S(1)}, f32[1024,128]{1,0:T(8,128)S(1)}, f32[1024,128]{1,0:T(8,128)S(1)}, f32[1024,128]{1,0:T(8,128)S(1)}) custom-call(f32[1024,128]{1,0:T(8,128)} %bitcast.12, f32[1024,128]{1,0:T(8,128)} %bitcast.13, f32[1024,128]{1,0:T(8,128)} %bitcast.14, f32[1024,128]{1,0:T(8,128)} %bitcast.15, ...), custom_call_target="tpu_custom_call" | custom-call | tf_op jit(solution)/shard_map/acoustic_substeps/pallas_call | solution.py:732
  59.7 0.0 copy-start
  59.7 0.8 %copy-done = f32[1024,128]{1,0:T(8,128)} copy-done((f32[1024,128]{1,0:T(8,128)}, f32[1024,128]{1,0:T(8,128)S(1)}, u32[]{:S(2)}) %copy-start) | copy-done | bytes 524312
  60.4 0.0 copy-start.1
  60.5 0.8 %copy-done.1 = f32[1024,128]{1,0:T(8,128)} copy-done((f32[1024,128]{1,0:T(8,128)}, f32[1024,128]{1,0:T(8,128)S(1)}, u32[]{:S(2)}) %copy-start.1) | copy-done | bytes 524312
  61.2 0.0 copy-start.2
  61.2 0.8 %copy-done.2 = f32[1024,128]{1,0:T(8,128)} copy-done((f32[1024,128]{1,0:T(8,128)}, f32[1024,128]{1,0:T(8,128)S(1)}, u32[]{:S(2)}) %copy-start.2) | copy-done | bytes 524312
  62.0 0.0 copy-start.3
  62.0 0.8 %copy-done.3 = f32[1024,128]{1,0:T(8,128)} copy-done((f32[1024,128]{1,0:T(8,128)}, f32[1024,128]{1,0:T(8,128)S(1)}, u32[]{:S(2)}) %copy-start.3) | copy-done | bytes 524312
  62.8 0.0 copy-start.4
  62.8 0.8 %copy-done.4 = f32[1024,128]{1,0:T(8,128)} copy-done((f32[1024,128]{1,0:T(8,128)}, f32[1024,128]{1,0:T(8,128)S(1)}, u32[]{:S(2)}) %copy-start.4) | copy-done | bytes 524312
  63.6 3.2 %store_outputs.1 = (f32[1024,128]{1,0:T(8,128)}, f32[1024,128]{1,0:T(8,128)}, f32[1024,128]{1,0:T(8,128)}, f32[1024,128]{1,0:T(8,128)}, f32[1024,128]{1,0:T(8,128)}) custom-call(f32[1024,128]{1,0:T(8,128)} %copy-done, f32[1024,128]{1,0:T(8,128)} %copy-done.1, f32[1024,128]{1,0:T(8,128)} %copy-done.2, f32[1024,128]{1,0:T(8,128)} %copy-done.3, ...), custom_call_target="tpu_custom_call" | custom-call | tf_op jit(solution)/shard_map/store_outputs/pallas_call | solution.py:754
Async XLA Ops:
  0.6 0.7 copy-start.5
  59.7 0.8 %copy-start = (f32[1024,128]{1,0:T(8,128)}, f32[1024,128]{1,0:T(8,128)S(1)}, u32[]{:S(2)}) copy-start(f32[1024,128]{1,0:T(8,128)S(1)} %get-tuple-element.15.a) | copy-start | bytes 1572868
  60.4 0.8 %copy-start.1 = (f32[1024,128]{1,0:T(8,128)}, f32[1024,128]{1,0:T(8,128)S(1)}, u32[]{:S(2)}) copy-start(f32[1024,128]{1,0:T(8,128)S(1)} %get-tuple-element.16.b) | copy-start | bytes 1572868
  61.2 0.8 %copy-start.2 = (f32[1024,128]{1,0:T(8,128)}, f32[1024,128]{1,0:T(8,128)S(1)}, u32[]{:S(2)}) copy-start(f32[1024,128]{1,0:T(8,128)S(1)} %get-tuple-element.17.c) | copy-start | bytes 1572868
  62.0 0.8 %copy-start.3 = (f32[1024,128]{1,0:T(8,128)}, f32[1024,128]{1,0:T(8,128)S(1)}, u32[]{:S(2)}) copy-start(f32[1024,128]{1,0:T(8,128)S(1)} %get-tuple-element.18.d) | copy-start | bytes 1572868
  62.8 0.8 %copy-start.4 = (f32[1024,128]{1,0:T(8,128)}, f32[1024,128]{1,0:T(8,128)S(1)}, u32[]{:S(2)}) copy-start(f32[1024,128]{1,0:T(8,128)S(1)} %get-tuple-element.19.e) | copy-start | bytes 1572868

commit v2 on v1

--- a/solution.py
+++ b/solution.py
@@ -233,7 +233,7 @@
     return (outputs[0], outputs[1], outputs[2], outputs[3], outputs[4])
 
 
-CHUNKS = 2
+CHUNKS = 4
 TILE = 8
 
 
@@ -304,11 +304,12 @@
 
 def fused(
     strips,
-    h_zon, h_mer, h_ver, h_pre, h_geo, h_lay, h_stf, inv_ref, ord_ref,
-    o_zon, o_mer, o_ver, o_pre, o_geo,
+    h_zon, h_mer, h_ver, h_pre, h_geo, h_lay, h_stf, h_ord,
+    q_zon, q_mer, q_ver, q_pre, q_geo,
     U, V, G, M, R, P, W, Z, C, I, H, A,
     s_m, r_m, s_uv, r_uv, s_w, r_w, s_d, r_d, s_g, r_g, s_e, r_e, r_a,
-    zon, mer, ver, pre, geo, lay, stf, send_sem, recv_sem, load_sem,
+    zon, mer, ver, pre, geo, lay, stf, ord_ref,
+    o_zon, o_mer, o_ver, o_pre, o_geo, send_sem, recv_sem, load_sem, store_sem,
 ):
     levels = U.shape[1]
     span = levels // CHUNKS
@@ -317,8 +318,7 @@
     lev = lax.axis_index("lev")
     left, right = lax.rem(me + strips - 1, strips), lax.rem(me + 1, strips)
     other = 1 - lev
-    inv = inv_ref[...]
-    order = ord_ref[...]
+    sequence = [c + lev * (CHUNKS - 1 - 2 * c) for c in range(CHUNKS)]
     quad = [1.0 / 6.0, 5.0 / 6.0, 5.0 / 6.0, 1.0 / 6.0]
     weights = [quad[n // 4] * quad[n % 4] for n in range(16)]
     started = []
@@ -387,6 +387,8 @@
         for copy in copies:
             copy.wait()
 
+    order_in = pltpu.make_async_copy(h_ord, ord_ref, load_sem.at[13])
+    order_in.start()
     lay_in, pre_in = fetch(h_lay, lay, 0), fetch(h_pre, pre, 1)
     ver_in, geo_in = fetch(h_ver, ver, 2), fetch(h_geo, geo, 3)
     zon_in, mer_in = fetch(h_zon, zon, 4), fetch(h_mer, mer, 5)
@@ -400,6 +402,15 @@
     pl.semaphore_wait(barrier, 3)
 
     stiff_copy = send(h_stf.at[pl.ds(pl.multiple_of(other * levels, 8), levels)], r_a, {"lev": other})
+
+    order_in.wait()
+    order = jnp.broadcast_to(ord_ref[...], (TILE, ord_ref.shape[1]))
+    lane = lax.broadcasted_iota(jnp.int32, order.shape, 1)
+    inv = jnp.zeros_like(order)
+    for turn in range(order.shape[1]):
+        moved = pltpu.roll(order, turn, 1) if turn else order
+        source = jnp.where(lane >= turn, lane - turn, lane - turn + order.shape[1])
+        inv = jnp.where(moved == lane, source, inv)
 
     def gather_rows(src, dst, c):
         def go(b, carry):
@@ -513,9 +524,11 @@
 
         each_tile(c, work)
 
+    stride = 16 - 32 * lev
+    outer = lev * ((levels - 1) * 16)
+
     def row(e):
-        k = e + lev * (levels - 1 - 2 * e)
-        return pl.ds(pl.multiple_of(k * 16, 16), 16)
+        return pl.ds(pl.multiple_of(outer + stride * e, 16), 16)
 
     side = (1 - 2 * lev).astype(jnp.float32)
     zero = jnp.zeros((16, P.shape[1]), jnp.float32)
@@ -550,40 +563,44 @@
         s_e[0, 1] = H[at, :] * I[at, :]
         return send(s_e.at[0], r_e.at[0], {"lev": other})
 
-    def eliminate(step):
+    def eliminate(step, c, carry):
         def one(e, before, here, after, z):
             at = row(e)
             z = (W[at, :] - H[at, :] * (after - before)) * I[at, :] + C[at, :] * z
             Z[at, :] = z
             return here, after, z
 
-        def go(block, carry):
+        def block(b, carry):
             before, here, z = carry
             for u in range(8):
-                e = block * 8 + u
-                after = P[row(e + 1), :]
-                before, here, z = one(e, before, here, after, z)
+                e = c * span + b * 8 + u - 1
+                before, here, z = one(e, before, here, P[row(e + 1), :], z)
             return before, here, z
 
-        carry = lax.fori_loop(0, levels // 8 - 1, go, (zero, P[row(0), :], zero))
+        if c == 0:
+            before, here, z = zero, P[row(0), :], zero
+            for u in range(7):
+                before, here, z = one(u, before, here, P[row(u + 1), :], z)
+            carry = (before, here, z)
+        carry = lax.fori_loop(1 if c == 0 else 0, tiles, block, carry)
+        if c < CHUNKS - 1:
+            return carry
         before, here, z = carry
-        for u in range(8):
-            e = levels - 8 + u
-            after = P[row(e + 1), :] if u < 7 else zero
-            before, here, z = one(e, before, here, after, z)
+        last, _, z = one(levels - 1, before, here, zero, z)
         s_e[step + 1, 0] = z
-        s_e[step + 1, 1] = before
+        s_e[step + 1, 1] = last
         return send(s_e.at[step + 1], r_e.at[step + 1], {"lev": other})
 
-    def substitute(step):
+    def interface(step):
         ratio, pull = s_e[0, 0], s_e[0, 1]
         ratio_other, pull_other = r_e[0, 0], r_e[0, 1]
         z = s_e[step + 1, 0] - pull * r_e[step + 1, 1]
         z_other = r_e[step + 1, 0] - pull_other * s_e[step + 1, 1]
         x = (z + ratio * z_other) / (1.0 - ratio * ratio_other)
-        beyond = z_other + ratio_other * x
         W[row(levels - 1), :] = x
-
+        return z_other + ratio_other * x, x
+
+    def substitute(c, carry):
         def one(e, beyond, x):
             here = Z[row(e), :] + C[row(e), :] * x
             W[row(e), :] = here
@@ -591,18 +608,18 @@
             P[at, :] = P[at, :] - H[at, :] * (beyond - here)
             return x, here
 
-        carry = (beyond, x)
-        for u in range(7):
-            carry = one(levels - 2 - u, *carry)
-
-        def go(block, carry):
+        def block(b, carry):
             for u in range(8):
-                carry = one(levels - 9 - block * 8 - u, *carry)
+                carry = one((c + 1) * span - 2 - b * 8 - u, *carry)
             return carry
 
-        beyond, x = lax.fori_loop(0, levels // 8 - 1, go, carry)
-        at = row(0)
-        P[at, :] = P[at, :] - H[at, :] * beyond
+        carry = lax.fori_loop(0, tiles - 1 if c == 0 else tiles, block, carry)
+        if c == 0:
+            for u in range(7):
+                carry = one(6 - u, *carry)
+            at = row(0)
+            P[at, :] = P[at, :] - H[at, :] * carry[0]
+        return carry
 
     def write_nodes(field, out, c):
         def work(l0, b0):
@@ -628,40 +645,58 @@
 
         lax.fori_loop(0, levels // TILE, go, 0)
 
+    stores = []
+
+    def store(src, dst):
+        copy = pltpu.make_async_copy(src, dst, store_sem.at[len(stores)])
+        copy.start()
+        stores.append(copy)
+
     edge_copy = None
+    solved = None
     for step in range(SUBSTEPS):
-        uv, w, d, g, m = [], [], [], [], []
+        uv, w, d, g, m = {}, {}, {}, {}, {}
+        for c in reversed(range(CHUNKS)):
+            at = sequence[c]
+            if step == 0:
+                if c == CHUNKS - 1:
+                    loaded(lay_in)
+                load_mass(at)
+                m[c] = send_faces(s_m, r_m, 0, at)
+                if c == CHUNKS - 1:
+                    loaded(pre_in)
+                gather_rows(pre, P, at)
+            else:
+                solved = substitute(c, solved)
+            wind_step(step, at)
+            uv[c] = send_faces(s_uv, r_uv, step, at)
+        if step == 0:
+            loaded(ver_in + geo_in)
         for c in range(CHUNKS):
+            at = sequence[c]
             if step == 0:
-                if c == 0:
-                    loaded(lay_in)
-                load_mass(c)
-                m.append(send_faces(s_m, r_m, 0, c))
-                if c == 0:
-                    loaded(pre_in)
-                gather_rows(pre, P, c)
-            wind_step(step, c)
-            uv.append(send_faces(s_uv, r_uv, step, c))
-        for c in range(CHUNKS):
-            if step == 0:
-                if c == 0:
-                    loaded(ver_in + geo_in)
-                gather_rows(ver, W, c)
-            vertical_step(step, c)
-            w.append(send_faces(s_w, r_w, step, c))
+                gather_rows(ver, W, at)
+            vertical_step(step, at)
+            w[c] = send_faces(s_w, r_w, step, at)
         if step == 0:
             loaded(zon_in + mer_in)
-            for c in range(CHUNKS):
-                start_winds(c)
+            for c in reversed(range(CHUNKS)):
+                start_winds(sequence[c])
+            for c in reversed(range(CHUNKS)):
                 arrive(m[c])
-                mass_faces(c)
+                mass_faces(sequence[c])
+        for c in reversed(range(CHUNKS)):
+            arrive(uv[c])
         for c in range(CHUNKS):
-            arrive(uv[c])
-            divergence_step(step, c)
-            d.append(send_faces(s_d, r_d, step, c))
+            divergence_step(step, sequence[c])
+            d[c] = send_faces(s_d, r_d, step, sequence[c])
         for c in range(CHUNKS):
-            geopotential_step(step, c)
-            g.append(send_faces(s_g, r_g, step, c))
+            if step > 0:
+                arrive(late[c])
+                geopotential_faces(step - 1, sequence[c])
+            geopotential_step(step, sequence[c])
+            g[c] = send_faces(s_g, r_g, step, sequence[c])
+        late = g
         if step == 0:
             stf_in.wait()
             stiff_copy.wait_recv()
@@ -670,38 +705,35 @@
             for c in range(CHUNKS):
                 write_nodes(U, o_zon, c)
                 write_nodes(V, o_mer, c)
+            store(o_zon, q_zon)
+            store(o_mer, q_mer)
+        carry = None
         for c in range(CHUNKS):
             arrive(w[c])
-            column_faces(W, s_w, r_w, step, c)
-        for c in range(CHUNKS):
+            column_faces(W, s_w, r_w, step, sequence[c])
             arrive(d[c])
-            column_faces(P, s_d, r_d, step, c)
-        message = eliminate(step)
-        for c in range(CHUNKS):
-            arrive(g[c])
-            geopotential_faces(step, c)
+            column_faces(P, s_d, r_d, step, sequence[c])
+            carry = eliminate(step, c, carry)
         if step == 0:
             edge_copy.wait_recv()
-        message.wait_recv()
-        substitute(step)
+        if step == SUBSTEPS - 1:
+            for c in range(CHUNKS):
+                arrive(late[c])
+                geopotential_faces(step, sequence[c])
+        carry.wait_recv()
+        solved = interface(step)
+    for c in reversed(range(CHUNKS)):
+        solved = substitute(c, solved)
+    write_rows(P, o_pre)
+    store(o_pre, q_pre)
+    write_rows(W, o_ver)
+    store(o_ver, q_ver)
     for c in range(CHUNKS):
         write_geopotential(c)
-    write_rows(W, o_ver)
-    write_rows(P, o_pre)
+    store(o_geo, q_geo)
     for copy in started:
         copy.wait_send()
-
-
-def store(a, b, c, d, e, p, q, r, s, t, sem):
-    copies = []
-    for src, dst in ((a, p), (b, q), (c, r), (d, s), (e, t)):
-        half = src.shape[0] // 2
-        for part in range(2):
-            rows = pl.ds(part * half, half)
-            copy = pltpu.make_async_copy(src.at[rows], dst.at[rows], sem.at[len(copies)])
-            copy.start()
-            copies.append(copy)
-    for copy in copies:
+    for copy in stores:
         copy.wait()
 
 
@@ -710,11 +742,6 @@
     stiffness, elem_order,
 ):
     levels, nodes, length = zonal_wind.shape
-    order = elem_order[0]
-    slots = jnp.arange(length, dtype=jnp.int32)
-    inverse = jnp.sum(jnp.where(order[:, None] == slots[None, :], slots[:, None], 0), axis=0)
-    inv = jnp.broadcast_to(inverse[None, :], (TILE, length))
-    back = jnp.broadcast_to(elem_order, (TILE, length))
     fields = [
         f.reshape(levels * nodes, length)
         for f in (zonal_wind, meridional_wind, vertical_wind, pressure, geopotential, layer_mass)
@@ -728,12 +755,12 @@
     level_major = pltpu.VMEM((levels * nodes, length), jnp.float32)
     edges = pltpu.VMEM((SUBSTEPS + 1, 2, nodes, length), jnp.float32)
     copies = 1 + 2 * CHUNKS + SUBSTEPS * 8 * CHUNKS + 1 + SUBSTEPS
-    vmem = pl.BlockSpec(memory_space=pltpu.VMEM)
+    anywhere = pl.BlockSpec(memory_space=pl.ANY)
     outputs = pl.pallas_call(
         functools.partial(fused, strips),
-        out_shape=[pltpu.VMEM((levels * nodes, length), jnp.float32)] * 5,
-        in_specs=[pl.BlockSpec(memory_space=pltpu.HBM)] * 7 + [vmem] * 2,
-        out_specs=[vmem] * 5,
+        out_shape=[jax.ShapeDtypeStruct((levels * nodes, length), jnp.float32)] * 5,
+        in_specs=[anywhere] * 8,
+        out_specs=[anywhere] * 5,
         scratch_shapes=[node_major] * 5
         + [level_major] * 7
         + faces(1, 3)
@@ -744,21 +771,15 @@
         + [edges, edges, pltpu.VMEM((levels, nodes // 2, length), jnp.float32)]
         + [level_major] * 6
         + [pltpu.VMEM((levels, nodes // 2, length), jnp.float32)]
+        + [pltpu.VMEM((1, length), jnp.int32)]
+        + [level_major] * 5
         + [pltpu.SemaphoreType.DMA((copies,)), pltpu.SemaphoreType.DMA((copies,))]
-        + [pltpu.SemaphoreType.DMA((13,))],
+        + [pltpu.SemaphoreType.DMA((14,)), pltpu.SemaphoreType.DMA((5,))],
         compiler_params=pltpu.CompilerParams(
             collective_id=0, has_side_effects=True, vmem_limit_bytes=52 * 1024 * 1024
         ),
         name="acoustic_substeps",
-    )(*fields, stiffness, inv, back)
-    outputs = pl.pallas_call(
-        store,
-        out_shape=[jax.ShapeDtypeStruct((levels * nodes, length), jnp.float32)] * 5,
-        in_specs=[vmem] * 5,
-        out_specs=[pl.BlockSpec(memory_space=pl.ANY)] * 5,
-        scratch_shapes=[pltpu.SemaphoreType.DMA((10,))],
-        name="store_outputs",
-    )(*outputs)
+    )(*fields, stiffness, elem_order)
     return tuple(f.reshape(levels, nodes, length) for f in outputs)
 
 

time: 67.1 us -> 66 us (0.984)
    broadcast_in_dim x2 -> x0, local copies, waits for them, and re-layouts: 1.19 us -> none  [the longest x1 0.6 us: pair_step(): inv = jnp.broadcast_to(inverse[None, :], (TILE, length))]
    unnamed x12 -> x11, local copies, waits for them, and re-layouts: 4.6 us -> 5.49 us
    pallas_call x2 -> x1, Pallas kernels: 60.3 us -> 59.7 us  [pair_step(): pl.pallas_call(functools.partial(fused, strips), out_shape=[jax.ShapeDtyp...]
where the time goes in v2:
time: 66 us; the launch traced here: 65.8 us
  Pallas kernels  59.7 us (90%)
  local copies, waits for them, and re-layouts  5.49 us (8%)
    pallas_call x1, Pallas kernels, pair_step(): pl.pallas_call(functools.partial(fused, strips), out_shape=[jax.ShapeDtyp...  59.7 us
    unnamed x11, local copies, waits for them, and re-layouts  5.49 us

profile of v2, /device:TPU:1, one launch (start us, length us, event | category | flops | bytes accessed | tf_op | source)
XLA Modules:
  0.0 65.8 jit_solution(17102666379063347826)
XLA Ops:
  0.6 0.0 copy-start
  0.6 0.6 copy-done
  1.3 59.7 %acoustic_substeps.1 = (f32[1024,128]{1,0:T(8,128)S(1)}, f32[1024,128]{1,0:T(8,128)S(1)}, f32[1024,128]{1,0:T(8,128)S(1)}, f32[1024,128]{1,0:T(8,128)}, f32[1024,128]{1,0:T(8,128)}) custom-call(f32[1024,128]{1,0:T(8,128)} %bitcast.16, f32[1024,128]{1,0:T(8,128)} %bitcast.17, f32[1024,128]{1,0:T(8,128)} %bitcast.18, f32[1024,128]{1,0:T(8,128)} %bitcast.19, ...), custom_call_target="tpu_custom_call" | custom-call | tf_op jit(solution)/shard_map/acoustic_substeps/pallas_call | solution.py:759
  61.0 0.8 %copy.18 = f32[64,16,128]{2,1,0:T(8,128)} copy(f32[64,16,128]{2,1,0:T(8,128)S(1)} %bitcast.13) | data formatting | bytes 1048576
  61.8 0.8 %copy.19 = f32[64,16,128]{2,1,0:T(8,128)} copy(f32[64,16,128]{2,1,0:T(8,128)S(1)} %bitcast.12) | data formatting | bytes 1048576
  62.5 0.0 copy-start.2
  62.5 0.8 %copy.20 = f32[64,16,128]{2,1,0:T(8,128)} copy(f32[64,16,128]{2,1,0:T(8,128)S(1)} %bitcast.11) | data formatting | bytes 1048576
  63.3 0.4 copy-done.2
  63.8 0.0 copy-start.1
  63.8 0.8 %copy.21 = f32[64,16,128]{2,1,0:T(8,128)} copy(f32[64,16,128]{2,1,0:T(8,128)S(1)} %bitcast.15) | data formatting | bytes 1048576
  64.6 0.4 copy-done.1
  65.0 0.8 %copy.22 = f32[64,16,128]{2,1,0:T(8,128)} copy(f32[64,16,128]{2,1,0:T(8,128)S(1)} %bitcast.14) | data formatting | bytes 1048576
Async XLA Ops:
  0.6 0.7 copy-start
  62.5 1.2 %copy-start.2 = (f32[1024,128]{1,0:T(8,128)S(1)}, f32[1024,128]{1,0:T(8,128)}, u32[]{:S(2)}) copy-start(f32[1024,128]{1,0:T(8,128)} %get-tuple-element.13) | copy-start | bytes 1572868
  63.8 1.2 %copy-start.1 = (f32[1024,128]{1,0:T(8,128)S(1)}, f32[1024,128]{1,0:T(8,128)}, u32[]{:S(2)}) copy-start(f32[1024,128]{1,0:T(8,128)} %get-tuple-element.14) | copy-start | bytes 1572868

commit v3 on v2

--- a/solution.py
+++ b/solution.py
@@ -233,7 +233,7 @@
     return (outputs[0], outputs[1], outputs[2], outputs[3], outputs[4])
 
 
-CHUNKS = 4
+CHUNKS = 2
 TILE = 8
 
 
@@ -776,7 +776,7 @@
         + [pltpu.SemaphoreType.DMA((copies,)), pltpu.SemaphoreType.DMA((copies,))]
         + [pltpu.SemaphoreType.DMA((14,)), pltpu.SemaphoreType.DMA((5,))],
         compiler_params=pltpu.CompilerParams(
-            collective_id=0, has_side_effects=True, vmem_limit_bytes=52 * 1024 * 1024
+            collective_id=0, has_side_effects=True, vmem_limit_bytes=58 * 1024 * 1024
         ),
         name="acoustic_substeps",
     )(*fields, stiffness, elem_order)

time: 66 us -> 67.5 us (1.023)
  local copies, waits for them, and re-layouts: 5.49 us -> 6.41 us
    unnamed x11 -> x13, local copies, waits for them, and re-layouts: 5.49 us -> 6.41 us
where the time goes in v3:
time: 67.5 us; the launch traced here: 67.2 us
  Pallas kernels  60.1 us (89%)
  local copies, waits for them, and re-layouts  6.41 us (9%)
    pallas_call x1, Pallas kernels, pair_step(): pl.pallas_call(functools.partial(fused, strips), out_shape=[jax.ShapeDtyp...  60.1 us
    unnamed x13, local copies, waits for them, and re-layouts  6.41 us

profile of v3, /device:TPU:1, one launch (start us, length us, event | category | flops | bytes accessed | tf_op | source)
XLA Modules:
  0.0 67.2 jit_solution(11959300718286982978)
XLA Ops:
  0.6 60.1 %acoustic_substeps.1 = (f32[1024,128]{1,0:T(8,128)}, f32[1024,128]{1,0:T(8,128)}, f32[1024,128]{1,0:T(8,128)}, f32[1024,128]{1,0:T(8,128)}, f32[1024,128]{1,0:T(8,128)}) custom-call(f32[1024,128]{1,0:T(8,128)} %bitcast.16, f32[1024,128]{1,0:T(8,128)} %bitcast.17, f32[1024,128]{1,0:T(8,128)} %bitcast.18, f32[1024,128]{1,0:T(8,128)} %bitcast.19, ...), custom_call_target="tpu_custom_call" | custom-call | tf_op jit(solution)/shard_map/acoustic_substeps/pallas_call | solution.py:759
  60.7 0.0 copy-start.3
  60.7 1.9 %copy.18 = f32[64,16,128]{2,1,0:T(8,128)} copy(f32[64,16,128]{2,1,0:T(8,128)} %bitcast.15) | data formatting | bytes 1048576
  62.7 0.0 copy-done.3
  62.7 0.0 copy-start.2
  62.7 0.8 %copy.19 = f32[64,16,128]{2,1,0:T(8,128)} copy(f32[64,16,128]{2,1,0:T(8,128)S(1)} %bitcast.14) | data formatting | bytes 1048576
  63.5 0.4 copy-done.2
  63.9 0.0 copy-start.1
  63.9 0.8 %copy.20 = f32[64,16,128]{2,1,0:T(8,128)} copy(f32[64,16,128]{2,1,0:T(8,128)S(1)} %bitcast.13) | data formatting | bytes 1048576
  64.7 0.4 copy-done.1
  65.1 0.0 copy-start
  65.1 0.8 %copy.21 = f32[64,16,128]{2,1,0:T(8,128)} copy(f32[64,16,128]{2,1,0:T(8,128)S(1)} %bitcast.12) | data formatting | bytes 1048576
  65.9 0.4 copy-done
  66.4 0.8 %copy.22 = f32[64,16,128]{2,1,0:T(8,128)} copy(f32[64,16,128]{2,1,0:T(8,128)S(1)} %bitcast.11) | data formatting | bytes 1048576
Async XLA Ops:
  60.7 1.9 %copy-start.3 = (f32[1024,128]{1,0:T(8,128)S(1)}, f32[1024,128]{1,0:T(8,128)}, u32[]{:S(2)}) copy-start(f32[1024,128]{1,0:T(8,128)} %get-tuple-element.11) | copy-start | bytes 1572868
  62.7 1.2 %copy-start.2 = (f32[1024,128]{1,0:T(8,128)S(1)}, f32[1024,128]{1,0:T(8,128)}, u32[]{:S(2)}) copy-start(f32[1024,128]{1,0:T(8,128)} %get-tuple-element.12) | copy-start | bytes 1572868
  63.9 1.2 %copy-start.1 = (f32[1024,128]{1,0:T(8,128)S(1)}, f32[1024,128]{1,0:T(8,128)}, u32[]{:S(2)}) copy-start(f32[1024,128]{1,0:T(8,128)} %get-tuple-element.13) | copy-start | bytes 1572868
  65.1 1.2 %copy-start = (f32[1024,128]{1,0:T(8,128)S(1)}, f32[1024,128]{1,0:T(8,128)}, u32[]{:S(2)}) copy-start(f32[1024,128]{1,0:T(8,128)} %get-tuple-element.14) | copy-start | bytes 1572868
